TPU v7x, 128 devices: a whole 4x4x4 slice. The times are simulated.
128 devices in a mesh: row: 8 (over z, x_lo), col: 16 (over x_hi, y, core).
Axes of the slice: x: 4 (x_hi: 2, x_lo: 2; x = x_hi * 2 + x_lo), y: 4, z: 4, core: 2. Of those that a mesh axis runs over, the one named last changes fastest.
Arguments:
- eigen_basis_rows: float32 [16384, 8192], P('row', 'col'), may hold values from -6 to 6
- mirror_entries: float32 [6, 8, 128, 2176], P(None, 'row', 'col'), may hold values from -0.125 to 0.125
- tau_coefficients: float32 [6, 8, 128], P(None, 'row', 'col'), may hold values from 0.5 to 2
- mirror_tallies: int32 [6, 8], P(None, 'row'), may hold values from 32 to 128
Outputs:
- transformed: float32 [16384, 8192], P('row', 'col')
All inputs are finite; a program needn't handle non-finite values.
Results may differ from a plain program's by a relative error of at most 0.00017.
Values sent between devices are 32-bit elements; how exact they have to be, the bound alone decides.
A program may use at most 64 MiB of HBM per device.

v0:
```python
import jax
import jax.numpy as jnp
from jax import lax
from jax.sharding import PartitionSpec as P

PRECISE = lax.Precision.HIGHEST


def shifted(block, axis, distance):
    devices = range(lax.axis_size(axis))
    route = [(i - distance, i) for i in devices if i - distance in devices]
    return lax.ppermute(block, axis, route)


def storage_triangle(mirror_directions, scaling, retention_flags):
    gram_matrix = lax.dot_general(
        mirror_directions,
        mirror_directions,
        (((1,), (1,)), ((), ())),
        precision=PRECISE,
        preferred_element_type=jnp.float32,
    )
    diag_inverse = jnp.where(retention_flags, scaling, jnp.ones_like(scaling))
    nilpotent = diag_inverse[:, None] * jnp.triu(gram_matrix, 1)
    order_count = mirror_directions.shape[0]
    identity = jnp.eye(order_count, dtype=jnp.float32)
    power_term = -nilpotent
    inverse_part = identity + power_term
    reached = 1
    while 2 * reached < order_count:
        power_term = jnp.dot(
            power_term, power_term, precision=PRECISE, preferred_element_type=jnp.float32
        )
        inverse_part = inverse_part + jnp.dot(
            inverse_part, power_term, precision=PRECISE, preferred_element_type=jnp.float32
        )
        reached = reached * 2
    return inverse_part * diag_inverse[None, :]


def apply_block(window, mirror_directions, triangle_operator):
    coeffs = jnp.dot(
        mirror_directions, window, precision=PRECISE, preferred_element_type=jnp.float32
    )
    mixed_terms = jnp.dot(
        triangle_operator, coeffs, precision=PRECISE, preferred_element_type=jnp.float32
    )
    return window - lax.dot_general(
        mirror_directions,
        mixed_terms,
        (((0,), (0,)), ((), ())),
        precision=PRECISE,
        preferred_element_type=jnp.float32,
    )


def per_device(eigen_basis_rows, mirror_entries, tau_coefficients, mirror_tallies):
    gathered, scale_all = (
        lax.all_gather(mirror_entries, "col", axis=2, tiled=True),
        lax.all_gather(tau_coefficients, "col", axis=2, tiled=True),
    )
    householders = gathered[:, 0]
    scale_rows = scale_all[:, 0]
    live_counts = mirror_tallies[:, 0]
    row_count = eigen_basis_rows.shape[0]
    group_count, width_rows, window_rows = householders.shape
    sections = lax.axis_size("row")
    position = lax.axis_index("row")
    slot_index = lax.iota(jnp.int32, width_rows)
    cell_index = lax.iota(jnp.int32, window_rows)
    retention_flags = slot_index[None, :] < live_counts[:, None]
    row_keep = (cell_index < row_count) | (position != sections - 1)
    householders = (
        householders
        * retention_flags[:, :, None].astype(jnp.float32)
        * row_keep[None, None, :].astype(jnp.float32)
    )
    factors = jax.vmap(storage_triangle)(householders, scale_rows, retention_flags)
    total_steps = 2 * (group_count - 1) + sections

    def plan(step_index, panel_ordinal):
        offset = step_index - panel_ordinal
        active = (offset >= 0) & (offset % 2 == 0) & (offset // 2 < group_count)
        return (active, jnp.clip(offset // 2, 0, group_count - 1))

    def advance(step_index, current):
        below_rows = shifted(current[:width_rows], "row", -1)
        active, batch_ordinal = plan(step_index, position)

        def working(state):
            window = jnp.concatenate([state, below_rows], axis=0)
            mirror_directions = lax.dynamic_index_in_dim(
                householders, batch_ordinal, 0, keepdims=False
            )
            triangle_operator = lax.dynamic_index_in_dim(factors, batch_ordinal, 0, keepdims=False)
            updated = apply_block(window, mirror_directions, triangle_operator)
            return (updated[:row_count], updated[row_count:])

        def waiting(state):
            return (state, below_rows)

        current, returned = lax.cond(active, working, waiting, current)
        arrived = shifted(returned, "row", 1)
        sender_active, unused = plan(step_index, position - 1)
        sender_active = sender_active & (position > 0)
        top_rows = jnp.where(sender_active, arrived, current[:width_rows])
        return lax.dynamic_update_slice_in_dim(current, top_rows, 0, 0)

    return lax.fori_loop(0, total_steps, advance, eigen_basis_rows)


def solution(mesh):
    in_specs = (P("row", "col"), P(None, "row", "col", None), P(None, "row", "col"), P(None, "row"))
    out_specs = P("row", "col")
    return jax.shard_map(
        per_device, mesh=mesh, in_specs=in_specs, out_specs=out_specs, check_vma=False
    )
```

profile of v0, /device:TPU:98, one launch (start us, length us, event | category | flops | bytes accessed | tf_op | source)
XLA Modules:
  0.0 718.3 jit_solution(6473481367738353305)
XLA Ops:
  6.5 4.7 copy.26
  11.4 23.7 %all_gather.7 = f32[6,1,128]{0,1,2:T(1,128)S(1)} all-gather(f32[6,1,8]{0,1,2:T(1,128)S(1)} %copy.8), channel_id=1, replica_groups=mesh['row'=8,'col'=16] {'col'}, dimensions={2}, use_global_device_ids=true | all-gather | bytes 3264 | tf_op jit(solution)/shard_map/all_gather | solution.py:60
  35.4 42.0 %all-gather.2.cloned.1.call-done = f32[6,1,128,2176]{3,2,0,1:T(8,128)} async-done(((f32[6,1,8,2176]{3,2,0,1:T(8,128)}), f32[6,1,128,2176]{3,2,0,1:T(8,128)}) %all-gather.2.cloned.1.call-update) | async-done | bytes 6684688 | tf_op jit(solution)/shard_map/all_gather | solution.py:59
  80.9 6.6 fusion.13
  94.1 617.3 %while.16 = (s32[]{:T(128)}, f32[2048,512]{1,0:T(8,128)}, s32[]{:T(128)}, f32[6,128,2176]{2,1,0:T(8,128)}, f32[6,128,128]{2,1,0:T(8,128)S(1)}, /*index=5*/s32[]{...) while((s32[]{:T(128)}, f32[2048,512]{1,0:T(8,128)}, s32[]{:T(128)}, ...), condition=%wide.region_3.4_spmd, body=%wide.region_0.3_spmd.sunk | while | flops 3524395008 | bytes 38470408 | solution.py:109
  98.5 5.9 collective-permute-done
  106.8 9.0 %collective-permute-done.1 = f32[128,512]{1,0:T(8,128)S(1)} collective-permute-done((f32[128,512]{1,0:T(8,128)S(1)}, f32[128,512]{1,0:T(8,128)S(1)}, u32[]{:S(2)}, u32[]{:S(2)}) %collective-permute-start.1) | collective-permute-done | bytes 262176 | tf_op jit(solution)/shard_map/while/body/eval_jaxpr/ppermute | solution.py:12
  117.4 4.6 collective-permute-start
  122.0 4.2 collective-permute-done
  128.6 7.4 %collective-permute-done.1 = f32[128,512]{1,0:T(8,128)S(1)} collective-permute-done((f32[128,512]{1,0:T(8,128)S(1)}, f32[128,512]{1,0:T(8,128)S(1)}, u32[]{:S(2)}, u32[]{:S(2)}) %collective-permute-start.1) | collective-permute-done | bytes 262176 | tf_op jit(solution)/shard_map/while/body/eval_jaxpr/ppermute | solution.py:12
  137.7 4.8 collective-permute-start
  148.7 7.4 %collective-permute-done.1 = f32[128,512]{1,0:T(8,128)S(1)} collective-permute-done((f32[128,512]{1,0:T(8,128)S(1)}, f32[128,512]{1,0:T(8,128)S(1)}, u32[]{:S(2)}, u32[]{:S(2)}) %collective-permute-start.1) | collective-permute-done | bytes 262176 | tf_op jit(solution)/shard_map/while/body/eval_jaxpr/ppermute | solution.py:12
  157.8 4.8 collective-permute-start
  168.8 13.5 %collective-permute-done.1 = f32[128,512]{1,0:T(8,128)S(1)} collective-permute-done((f32[128,512]{1,0:T(8,128)S(1)}, f32[128,512]{1,0:T(8,128)S(1)}, u32[]{:S(2)}, u32[]{:S(2)}) %collective-permute-start.1) | collective-permute-done | bytes 262176 | tf_op jit(solution)/shard_map/while/body/eval_jaxpr/ppermute | solution.py:12
  184.0 18.7 %collective-permute-start = (f32[128,512]{1,0:T(8,128)S(1)}, f32[128,512]{1,0:T(8,128)S(1)}, u32[]{:S(2)}, u32[]{:S(2)}) collective-permute-start(f32[128,512]{1,0:T(8,128)S(1)} %slice.40), channel_id=1, source_target_pairs={{16,0},{32,16},{48,32},{64,48},{80,64},{96,80},{112,96},{17,1},{33... | collective-permute-start | bytes 786440 | tf_op jit(solution)/shard_map/while/body/eval_jaxpr/ppermute | solution.py:12
  208.9 21.9 %collective-permute-done.1 = f32[128,512]{1,0:T(8,128)S(1)} collective-permute-done((f32[128,512]{1,0:T(8,128)S(1)}, f32[128,512]{1,0:T(8,128)S(1)}, u32[]{:S(2)}, u32[]{:S(2)}) %collective-permute-start.1) | collective-permute-done | bytes 262176 | tf_op jit(solution)/shard_map/while/body/eval_jaxpr/ppermute | solution.py:12
  232.5 20.5 %collective-permute-start = (f32[128,512]{1,0:T(8,128)S(1)}, f32[128,512]{1,0:T(8,128)S(1)}, u32[]{:S(2)}, u32[]{:S(2)}) collective-permute-start(f32[128,512]{1,0:T(8,128)S(1)} %slice.40), channel_id=1, source_target_pairs={{16,0},{32,16},{48,32},{64,48},{80,64},{96,80},{112,96},{17,1},{33... | collective-permute-start | bytes 786440 | tf_op jit(solution)/shard_map/while/body/eval_jaxpr/ppermute | solution.py:12
  259.3 21.7 %collective-permute-done.1 = f32[128,512]{1,0:T(8,128)S(1)} collective-permute-done((f32[128,512]{1,0:T(8,128)S(1)}, f32[128,512]{1,0:T(8,128)S(1)}, u32[]{:S(2)}, u32[]{:S(2)}) %collective-permute-start.1) | collective-permute-done | bytes 262176 | tf_op jit(solution)/shard_map/while/body/eval_jaxpr/ppermute | solution.py:12
  282.7 18.7 %collective-permute-start = (f32[128,512]{1,0:T(8,128)S(1)}, f32[128,512]{1,0:T(8,128)S(1)}, u32[]{:S(2)}, u32[]{:S(2)}) collective-permute-start(f32[128,512]{1,0:T(8,128)S(1)} %slice.40), channel_id=1, source_target_pairs={{16,0},{32,16},{48,32},{64,48},{80,64},{96,80},{112,96},{17,1},{33... | collective-permute-start | bytes 786440 | tf_op jit(solution)/shard_map/while/body/eval_jaxpr/ppermute | solution.py:12
  307.6 21.6 %collective-permute-done.1 = f32[128,512]{1,0:T(8,128)S(1)} collective-permute-done((f32[128,512]{1,0:T(8,128)S(1)}, f32[128,512]{1,0:T(8,128)S(1)}, u32[]{:S(2)}, u32[]{:S(2)}) %collective-permute-start.1) | collective-permute-done | bytes 262176 | tf_op jit(solution)/shard_map/while/body/eval_jaxpr/ppermute | solution.py:12
  331.0 4.8 collective-permute-start
  339.7 14.4 %conditional.2 = (f32[2048,512]{1,0:T(8,128)}, f32[128,512]{1,0:T(8,128)S(1)}, f32[128,512]{1,0:T(8,128)S(1)}) conditional(s32[]{:T(128)} %convert_element_type.41, (f32[2048,512]{1,0:T(8,128)}, f32[128,512]{1,0:T(8,128)S(1)}) %tuple.59, (f32[2048,512]{1,0:T(8,128)}, f32[128,512]{1,0:T(8,128)S(1)}, s32[]{:T(128)}, f32[6,128,2176]{2,1,0:T(8,128)}, ...), branch_computations={%region_1.1_spmd, %region_2.2_spmd} | conditional | flops 3524329472 | bytes 35061820 | solution.py:102
  342.3 3.9 fusion.1
  346.6 5.0 convolution_subtract_fusion
  355.4 6.9 collective-permute-done.1
  364.0 6.0 collective-permute-start
  376.2 20.8 %collective-permute-done.1 = f32[128,512]{1,0:T(8,128)S(1)} collective-permute-done((f32[128,512]{1,0:T(8,128)S(1)}, f32[128,512]{1,0:T(8,128)S(1)}, u32[]{:S(2)}, u32[]{:S(2)}) %collective-permute-start.1) | collective-permute-done | bytes 262176 | tf_op jit(solution)/shard_map/while/body/eval_jaxpr/ppermute | solution.py:12
  398.7 4.8 collective-permute-start
  407.4 14.4 %conditional.2 = (f32[2048,512]{1,0:T(8,128)}, f32[128,512]{1,0:T(8,128)S(1)}, f32[128,512]{1,0:T(8,128)S(1)}) conditional(s32[]{:T(128)} %convert_element_type.41, (f32[2048,512]{1,0:T(8,128)}, f32[128,512]{1,0:T(8,128)S(1)}) %tuple.59, (f32[2048,512]{1,0:T(8,128)}, f32[128,512]{1,0:T(8,128)S(1)}, s32[]{:T(128)}, f32[6,128,2176]{2,1,0:T(8,128)}, ...), branch_computations={%region_1.1_spmd, %region_2.2_spmd} | conditional | flops 3524329472 | bytes 35061820 | solution.py:102
  410.1 3.9 fusion.1
  414.3 5.0 convolution_subtract_fusion
  423.2 6.9 collective-permute-done.1
  431.8 5.5 collective-permute-start
  443.5 20.8 %collective-permute-done.1 = f32[128,512]{1,0:T(8,128)S(1)} collective-permute-done((f32[128,512]{1,0:T(8,128)S(1)}, f32[128,512]{1,0:T(8,128)S(1)}, u32[]{:S(2)}, u32[]{:S(2)}) %collective-permute-start.1) | collective-permute-done | bytes 262176 | tf_op jit(solution)/shard_map/while/body/eval_jaxpr/ppermute | solution.py:12
  466.1 4.8 collective-permute-start
  470.9 4.3 collective-permute-done
  475.3 14.4 %conditional.2 = (f32[2048,512]{1,0:T(8,128)}, f32[128,512]{1,0:T(8,128)S(1)}, f32[128,512]{1,0:T(8,128)S(1)}) conditional(s32[]{:T(128)} %convert_element_type.41, (f32[2048,512]{1,0:T(8,128)}, f32[128,512]{1,0:T(8,128)S(1)}) %tuple.59, (f32[2048,512]{1,0:T(8,128)}, f32[128,512]{1,0:T(8,128)S(1)}, s32[]{:T(128)}, f32[6,128,2176]{2,1,0:T(8,128)}, ...), branch_computations={%region_1.1_spmd, %region_2.2_spmd} | conditional | flops 3524329472 | bytes 35061820 | solution.py:102
  477.9 3.9 fusion.1
  482.2 5.0 convolution_subtract_fusion
  491.0 7.8 %collective-permute-done.1 = f32[128,512]{1,0:T(8,128)S(1)} collective-permute-done((f32[128,512]{1,0:T(8,128)S(1)}, f32[128,512]{1,0:T(8,128)S(1)}, u32[]{:S(2)}, u32[]{:S(2)}) %collective-permute-start.1) | collective-permute-done | bytes 262176 | tf_op jit(solution)/shard_map/while/body/eval_jaxpr/ppermute | solution.py:12
  500.5 4.2 collective-permute-start
  504.8 5.7 collective-permute-done
  512.8 23.2 %collective-permute-done.1 = f32[128,512]{1,0:T(8,128)S(1)} collective-permute-done((f32[128,512]{1,0:T(8,128)S(1)}, f32[128,512]{1,0:T(8,128)S(1)}, u32[]{:S(2)}, u32[]{:S(2)}) %collective-permute-start.1) | collective-permute-done | bytes 262176 | tf_op jit(solution)/shard_map/while/body/eval_jaxpr/ppermute | solution.py:12
  537.8 6.4 collective-permute-start
  544.2 5.6 collective-permute-done
  549.8 14.4 %conditional.2 = (f32[2048,512]{1,0:T(8,128)}, f32[128,512]{1,0:T(8,128)S(1)}, f32[128,512]{1,0:T(8,128)S(1)}) conditional(s32[]{:T(128)} %convert_element_type.41, (f32[2048,512]{1,0:T(8,128)}, f32[128,512]{1,0:T(8,128)S(1)}) %tuple.59, (f32[2048,512]{1,0:T(8,128)}, f32[128,512]{1,0:T(8,128)S(1)}, s32[]{:T(128)}, f32[6,128,2176]{2,1,0:T(8,128)}, ...), branch_computations={%region_1.1_spmd, %region_2.2_spmd} | conditional | flops 3524329472 | bytes 35061820 | solution.py:102
  552.5 3.9 fusion.1
  556.7 5.0 convolution_subtract_fusion
  565.6 8.5 %collective-permute-done.1 = f32[128,512]{1,0:T(8,128)S(1)} collective-permute-done((f32[128,512]{1,0:T(8,128)S(1)}, f32[128,512]{1,0:T(8,128)S(1)}, u32[]{:S(2)}, u32[]{:S(2)}) %collective-permute-start.1) | collective-permute-done | bytes 262176 | tf_op jit(solution)/shard_map/while/body/eval_jaxpr/ppermute | solution.py:12
  575.8 4.6 collective-permute-start
  580.4 5.6 collective-permute-done
  588.3 21.2 %collective-permute-done.1 = f32[128,512]{1,0:T(8,128)S(1)} collective-permute-done((f32[128,512]{1,0:T(8,128)S(1)}, f32[128,512]{1,0:T(8,128)S(1)}, u32[]{:S(2)}, u32[]{:S(2)}) %collective-permute-start.1) | collective-permute-done | bytes 262176 | tf_op jit(solution)/shard_map/while/body/eval_jaxpr/ppermute | solution.py:12
  611.2 4.4 collective-permute-start
  619.5 14.4 %conditional.2 = (f32[2048,512]{1,0:T(8,128)}, f32[128,512]{1,0:T(8,128)S(1)}, f32[128,512]{1,0:T(8,128)S(1)}) conditional(s32[]{:T(128)} %convert_element_type.41, (f32[2048,512]{1,0:T(8,128)}, f32[128,512]{1,0:T(8,128)S(1)}) %tuple.59, (f32[2048,512]{1,0:T(8,128)}, f32[128,512]{1,0:T(8,128)S(1)}, s32[]{:T(128)}, f32[6,128,2176]{2,1,0:T(8,128)}, ...), branch_computations={%region_1.1_spmd, %region_2.2_spmd} | conditional | flops 3524329472 | bytes 35061820 | solution.py:102
  622.2 3.9 fusion.1
  626.4 5.0 convolution_subtract_fusion
  635.3 9.1 %collective-permute-done.1 = f32[128,512]{1,0:T(8,128)S(1)} collective-permute-done((f32[128,512]{1,0:T(8,128)S(1)}, f32[128,512]{1,0:T(8,128)S(1)}, u32[]{:S(2)}, u32[]{:S(2)}) %collective-permute-start.1) | collective-permute-done | bytes 262176 | tf_op jit(solution)/shard_map/while/body/eval_jaxpr/ppermute | solution.py:12
  646.1 4.6 collective-permute-start
  656.8 20.8 %collective-permute-done.1 = f32[128,512]{1,0:T(8,128)S(1)} collective-permute-done((f32[128,512]{1,0:T(8,128)S(1)}, f32[128,512]{1,0:T(8,128)S(1)}, u32[]{:S(2)}, u32[]{:S(2)}) %collective-permute-start.1) | collective-permute-done | bytes 262176 | tf_op jit(solution)/shard_map/while/body/eval_jaxpr/ppermute | solution.py:12
  679.3 4.8 collective-permute-start
  688.0 14.4 %conditional.2 = (f32[2048,512]{1,0:T(8,128)}, f32[128,512]{1,0:T(8,128)S(1)}, f32[128,512]{1,0:T(8,128)S(1)}) conditional(s32[]{:T(128)} %convert_element_type.41, (f32[2048,512]{1,0:T(8,128)}, f32[128,512]{1,0:T(8,128)S(1)}) %tuple.59, (f32[2048,512]{1,0:T(8,128)}, f32[128,512]{1,0:T(8,128)S(1)}, s32[]{:T(128)}, f32[6,128,2176]{2,1,0:T(8,128)}, ...), branch_computations={%region_1.1_spmd, %region_2.2_spmd} | conditional | flops 3524329472 | bytes 35061820 | solution.py:102
  690.7 3.9 fusion.1
  694.9 5.0 convolution_subtract_fusion
  703.8 6.9 collective-permute-done.1
  (152 shorter events, 169.8 us)
Async XLA Ops:
  6.5 4.7 copy-start.1
  6.5 4.8 copy-start.2
  6.5 70.9 %all-gather.2.cloned.1.call-start = ((), (), s32[]{:S(2)}) async-start(), calls=%async_computation | async-start | bytes 7102464 | tf_op jit(solution)/shard_map/all_gather | solution.py:59
  80.9 6.6 copy-start
  95.1 9.3 %collective-permute-start = (f32[128,512]{1,0:T(8,128)S(1)}, f32[128,512]{1,0:T(8,128)S(1)}, u32[]{:S(2)}, u32[]{:S(2)}) collective-permute-start(f32[128,512]{1,0:T(8,128)S(1)} %slice.40), channel_id=1, source_target_pairs={{16,0},{32,16},{48,32},{64,48},{80,64},{96,80},{112,96},{17,1},{33... | collective-permute-start | bytes 786440 | tf_op jit(solution)/shard_map/while/body/eval_jaxpr/ppermute | solution.py:12
  105.4 10.3 %collective-permute-start.1 = (f32[128,512]{1,0:T(8,128)S(1)}, f32[128,512]{1,0:T(8,128)S(1)}, u32[]{:S(2)}, u32[]{:S(2)}) collective-permute-start(f32[128,512]{1,0:T(8,128)S(1)} %get-tuple-element.288), channel_id=1, source_target_pairs={{0,16},{16,32},{32,48},{48,64},{64,80},{80,96},{96,112},{1,17},{17... | collective-permute-start | bytes 786440 | tf_op jit(solution)/shard_map/while/body/eval_jaxpr/ppermute | solution.py:12
  117.4 8.8 %collective-permute-start = (f32[128,512]{1,0:T(8,128)S(1)}, f32[128,512]{1,0:T(8,128)S(1)}, u32[]{:S(2)}, u32[]{:S(2)}) collective-permute-start(f32[128,512]{1,0:T(8,128)S(1)} %slice.40), channel_id=1, source_target_pairs={{16,0},{32,16},{48,32},{64,48},{80,64},{96,80},{112,96},{17,1},{33... | collective-permute-start | bytes 786440 | tf_op jit(solution)/shard_map/while/body/eval_jaxpr/ppermute | solution.py:12
  127.2 8.7 %collective-permute-start.1 = (f32[128,512]{1,0:T(8,128)S(1)}, f32[128,512]{1,0:T(8,128)S(1)}, u32[]{:S(2)}, u32[]{:S(2)}) collective-permute-start(f32[128,512]{1,0:T(8,128)S(1)} %get-tuple-element.288), channel_id=1, source_target_pairs={{0,16},{16,32},{32,48},{48,64},{64,80},{80,96},{96,112},{1,17},{17... | collective-permute-start | bytes 786440 | tf_op jit(solution)/shard_map/while/body/eval_jaxpr/ppermute | solution.py:12
  137.7 8.7 %collective-permute-start = (f32[128,512]{1,0:T(8,128)S(1)}, f32[128,512]{1,0:T(8,128)S(1)}, u32[]{:S(2)}, u32[]{:S(2)}) collective-permute-start(f32[128,512]{1,0:T(8,128)S(1)} %slice.40), channel_id=1, source_target_pairs={{16,0},{32,16},{48,32},{64,48},{80,64},{96,80},{112,96},{17,1},{33... | collective-permute-start | bytes 786440 | tf_op jit(solution)/shard_map/while/body/eval_jaxpr/ppermute | solution.py:12
  147.3 8.7 %collective-permute-start.1 = (f32[128,512]{1,0:T(8,128)S(1)}, f32[128,512]{1,0:T(8,128)S(1)}, u32[]{:S(2)}, u32[]{:S(2)}) collective-permute-start(f32[128,512]{1,0:T(8,128)S(1)} %get-tuple-element.288), channel_id=1, source_target_pairs={{0,16},{16,32},{32,48},{48,64},{64,80},{80,96},{96,112},{1,17},{17... | collective-permute-start | bytes 786440 | tf_op jit(solution)/shard_map/while/body/eval_jaxpr/ppermute | solution.py:12
  157.8 8.7 %collective-permute-start = (f32[128,512]{1,0:T(8,128)S(1)}, f32[128,512]{1,0:T(8,128)S(1)}, u32[]{:S(2)}, u32[]{:S(2)}) collective-permute-start(f32[128,512]{1,0:T(8,128)S(1)} %slice.40), channel_id=1, source_target_pairs={{16,0},{32,16},{48,32},{64,48},{80,64},{96,80},{112,96},{17,1},{33... | collective-permute-start | bytes 786440 | tf_op jit(solution)/shard_map/while/body/eval_jaxpr/ppermute | solution.py:12
  167.5 14.8 %collective-permute-start.1 = (f32[128,512]{1,0:T(8,128)S(1)}, f32[128,512]{1,0:T(8,128)S(1)}, u32[]{:S(2)}, u32[]{:S(2)}) collective-permute-start(f32[128,512]{1,0:T(8,128)S(1)} %get-tuple-element.288), channel_id=1, source_target_pairs={{0,16},{16,32},{32,48},{48,64},{64,80},{80,96},{96,112},{1,17},{17... | collective-permute-start | bytes 786440 | tf_op jit(solution)/shard_map/while/body/eval_jaxpr/ppermute | solution.py:12
  184.0 22.6 %collective-permute-start = (f32[128,512]{1,0:T(8,128)S(1)}, f32[128,512]{1,0:T(8,128)S(1)}, u32[]{:S(2)}, u32[]{:S(2)}) collective-permute-start(f32[128,512]{1,0:T(8,128)S(1)} %slice.40), channel_id=1, source_target_pairs={{16,0},{32,16},{48,32},{64,48},{80,64},{96,80},{112,96},{17,1},{33... | collective-permute-start | bytes 786440 | tf_op jit(solution)/shard_map/while/body/eval_jaxpr/ppermute | solution.py:12
  207.6 23.3 %collective-permute-start.1 = (f32[128,512]{1,0:T(8,128)S(1)}, f32[128,512]{1,0:T(8,128)S(1)}, u32[]{:S(2)}, u32[]{:S(2)}) collective-permute-start(f32[128,512]{1,0:T(8,128)S(1)} %get-tuple-element.288), channel_id=1, source_target_pairs={{0,16},{16,32},{32,48},{48,64},{64,80},{80,96},{96,112},{1,17},{17... | collective-permute-start | bytes 786440 | tf_op jit(solution)/shard_map/while/body/eval_jaxpr/ppermute | solution.py:12
  232.5 24.4 %collective-permute-start = (f32[128,512]{1,0:T(8,128)S(1)}, f32[128,512]{1,0:T(8,128)S(1)}, u32[]{:S(2)}, u32[]{:S(2)}) collective-permute-start(f32[128,512]{1,0:T(8,128)S(1)} %slice.40), channel_id=1, source_target_pairs={{16,0},{32,16},{48,32},{64,48},{80,64},{96,80},{112,96},{17,1},{33... | collective-permute-start | bytes 786440 | tf_op jit(solution)/shard_map/while/body/eval_jaxpr/ppermute | solution.py:12
  257.9 23.1 %collective-permute-start.1 = (f32[128,512]{1,0:T(8,128)S(1)}, f32[128,512]{1,0:T(8,128)S(1)}, u32[]{:S(2)}, u32[]{:S(2)}) collective-permute-start(f32[128,512]{1,0:T(8,128)S(1)} %get-tuple-element.288), channel_id=1, source_target_pairs={{0,16},{16,32},{32,48},{48,64},{64,80},{80,96},{96,112},{1,17},{17... | collective-permute-start | bytes 786440 | tf_op jit(solution)/shard_map/while/body/eval_jaxpr/ppermute | solution.py:12
  282.7 22.6 %collective-permute-start = (f32[128,512]{1,0:T(8,128)S(1)}, f32[128,512]{1,0:T(8,128)S(1)}, u32[]{:S(2)}, u32[]{:S(2)}) collective-permute-start(f32[128,512]{1,0:T(8,128)S(1)} %slice.40), channel_id=1, source_target_pairs={{16,0},{32,16},{48,32},{64,48},{80,64},{96,80},{112,96},{17,1},{33... | collective-permute-start | bytes 786440 | tf_op jit(solution)/shard_map/while/body/eval_jaxpr/ppermute | solution.py:12
  306.3 23.0 %collective-permute-start.1 = (f32[128,512]{1,0:T(8,128)S(1)}, f32[128,512]{1,0:T(8,128)S(1)}, u32[]{:S(2)}, u32[]{:S(2)}) collective-permute-start(f32[128,512]{1,0:T(8,128)S(1)} %get-tuple-element.288), channel_id=1, source_target_pairs={{0,16},{16,32},{32,48},{48,64},{64,80},{80,96},{96,112},{1,17},{17... | collective-permute-start | bytes 786440 | tf_op jit(solution)/shard_map/while/body/eval_jaxpr/ppermute | solution.py:12
  331.0 8.7 %collective-permute-start = (f32[128,512]{1,0:T(8,128)S(1)}, f32[128,512]{1,0:T(8,128)S(1)}, u32[]{:S(2)}, u32[]{:S(2)}) collective-permute-start(f32[128,512]{1,0:T(8,128)S(1)} %slice.40), channel_id=1, source_target_pairs={{16,0},{32,16},{48,32},{64,48},{80,64},{96,80},{112,96},{17,1},{33... | collective-permute-start | bytes 786440 | tf_op jit(solution)/shard_map/while/body/eval_jaxpr/ppermute | solution.py:12
  354.1 8.3 %collective-permute-start.1 = (f32[128,512]{1,0:T(8,128)S(1)}, f32[128,512]{1,0:T(8,128)S(1)}, u32[]{:S(2)}, u32[]{:S(2)}) collective-permute-start(f32[128,512]{1,0:T(8,128)S(1)} %get-tuple-element.288), channel_id=1, source_target_pairs={{0,16},{16,32},{32,48},{48,64},{64,80},{80,96},{96,112},{1,17},{17... | collective-permute-start | bytes 786440 | tf_op jit(solution)/shard_map/while/body/eval_jaxpr/ppermute | solution.py:12
  364.0 9.8 %collective-permute-start = (f32[128,512]{1,0:T(8,128)S(1)}, f32[128,512]{1,0:T(8,128)S(1)}, u32[]{:S(2)}, u32[]{:S(2)}) collective-permute-start(f32[128,512]{1,0:T(8,128)S(1)} %slice.40), channel_id=1, source_target_pairs={{16,0},{32,16},{48,32},{64,48},{80,64},{96,80},{112,96},{17,1},{33... | collective-permute-start | bytes 786440 | tf_op jit(solution)/shard_map/while/body/eval_jaxpr/ppermute | solution.py:12
  374.9 22.2 %collective-permute-start.1 = (f32[128,512]{1,0:T(8,128)S(1)}, f32[128,512]{1,0:T(8,128)S(1)}, u32[]{:S(2)}, u32[]{:S(2)}) collective-permute-start(f32[128,512]{1,0:T(8,128)S(1)} %get-tuple-element.288), channel_id=1, source_target_pairs={{0,16},{16,32},{32,48},{48,64},{64,80},{80,96},{96,112},{1,17},{17... | collective-permute-start | bytes 786440 | tf_op jit(solution)/shard_map/while/body/eval_jaxpr/ppermute | solution.py:12
  398.7 8.7 %collective-permute-start = (f32[128,512]{1,0:T(8,128)S(1)}, f32[128,512]{1,0:T(8,128)S(1)}, u32[]{:S(2)}, u32[]{:S(2)}) collective-permute-start(f32[128,512]{1,0:T(8,128)S(1)} %slice.40), channel_id=1, source_target_pairs={{16,0},{32,16},{48,32},{64,48},{80,64},{96,80},{112,96},{17,1},{33... | collective-permute-start | bytes 786440 | tf_op jit(solution)/shard_map/while/body/eval_jaxpr/ppermute | solution.py:12
  421.8 8.3 %collective-permute-start.1 = (f32[128,512]{1,0:T(8,128)S(1)}, f32[128,512]{1,0:T(8,128)S(1)}, u32[]{:S(2)}, u32[]{:S(2)}) collective-permute-start(f32[128,512]{1,0:T(8,128)S(1)} %get-tuple-element.288), channel_id=1, source_target_pairs={{0,16},{16,32},{32,48},{48,64},{64,80},{80,96},{96,112},{1,17},{17... | collective-permute-start | bytes 786440 | tf_op jit(solution)/shard_map/while/body/eval_jaxpr/ppermute | solution.py:12
  431.8 9.4 %collective-permute-start = (f32[128,512]{1,0:T(8,128)S(1)}, f32[128,512]{1,0:T(8,128)S(1)}, u32[]{:S(2)}, u32[]{:S(2)}) collective-permute-start(f32[128,512]{1,0:T(8,128)S(1)} %slice.40), channel_id=1, source_target_pairs={{16,0},{32,16},{48,32},{64,48},{80,64},{96,80},{112,96},{17,1},{33... | collective-permute-start | bytes 786440 | tf_op jit(solution)/shard_map/while/body/eval_jaxpr/ppermute | solution.py:12
  442.2 22.2 %collective-permute-start.1 = (f32[128,512]{1,0:T(8,128)S(1)}, f32[128,512]{1,0:T(8,128)S(1)}, u32[]{:S(2)}, u32[]{:S(2)}) collective-permute-start(f32[128,512]{1,0:T(8,128)S(1)} %get-tuple-element.288), channel_id=1, source_target_pairs={{0,16},{16,32},{32,48},{48,64},{64,80},{80,96},{96,112},{1,17},{17... | collective-permute-start | bytes 786440 | tf_op jit(solution)/shard_map/while/body/eval_jaxpr/ppermute | solution.py:12
  466.1 9.2 %collective-permute-start = (f32[128,512]{1,0:T(8,128)S(1)}, f32[128,512]{1,0:T(8,128)S(1)}, u32[]{:S(2)}, u32[]{:S(2)}) collective-permute-start(f32[128,512]{1,0:T(8,128)S(1)} %slice.40), channel_id=1, source_target_pairs={{16,0},{32,16},{48,32},{64,48},{80,64},{96,80},{112,96},{17,1},{33... | collective-permute-start | bytes 786440 | tf_op jit(solution)/shard_map/while/body/eval_jaxpr/ppermute | solution.py:12
  489.7 9.1 %collective-permute-start.1 = (f32[128,512]{1,0:T(8,128)S(1)}, f32[128,512]{1,0:T(8,128)S(1)}, u32[]{:S(2)}, u32[]{:S(2)}) collective-permute-start(f32[128,512]{1,0:T(8,128)S(1)} %get-tuple-element.288), channel_id=1, source_target_pairs={{0,16},{16,32},{32,48},{48,64},{64,80},{80,96},{96,112},{1,17},{17... | collective-permute-start | bytes 786440 | tf_op jit(solution)/shard_map/while/body/eval_jaxpr/ppermute | solution.py:12
  500.5 10.0 %collective-permute-start = (f32[128,512]{1,0:T(8,128)S(1)}, f32[128,512]{1,0:T(8,128)S(1)}, u32[]{:S(2)}, u32[]{:S(2)}) collective-permute-start(f32[128,512]{1,0:T(8,128)S(1)} %slice.40), channel_id=1, source_target_pairs={{16,0},{32,16},{48,32},{64,48},{80,64},{96,80},{112,96},{17,1},{33... | collective-permute-start | bytes 786440 | tf_op jit(solution)/shard_map/while/body/eval_jaxpr/ppermute | solution.py:12
  511.5 24.6 %collective-permute-start.1 = (f32[128,512]{1,0:T(8,128)S(1)}, f32[128,512]{1,0:T(8,128)S(1)}, u32[]{:S(2)}, u32[]{:S(2)}) collective-permute-start(f32[128,512]{1,0:T(8,128)S(1)} %get-tuple-element.288), channel_id=1, source_target_pairs={{0,16},{16,32},{32,48},{48,64},{64,80},{80,96},{96,112},{1,17},{17... | collective-permute-start | bytes 786440 | tf_op jit(solution)/shard_map/while/body/eval_jaxpr/ppermute | solution.py:12
  537.8 12.0 %collective-permute-start = (f32[128,512]{1,0:T(8,128)S(1)}, f32[128,512]{1,0:T(8,128)S(1)}, u32[]{:S(2)}, u32[]{:S(2)}) collective-permute-start(f32[128,512]{1,0:T(8,128)S(1)} %slice.40), channel_id=1, source_target_pairs={{16,0},{32,16},{48,32},{64,48},{80,64},{96,80},{112,96},{17,1},{33... | collective-permute-start | bytes 786440 | tf_op jit(solution)/shard_map/while/body/eval_jaxpr/ppermute | solution.py:12
  564.2 9.9 %collective-permute-start.1 = (f32[128,512]{1,0:T(8,128)S(1)}, f32[128,512]{1,0:T(8,128)S(1)}, u32[]{:S(2)}, u32[]{:S(2)}) collective-permute-start(f32[128,512]{1,0:T(8,128)S(1)} %get-tuple-element.288), channel_id=1, source_target_pairs={{0,16},{16,32},{32,48},{48,64},{64,80},{80,96},{96,112},{1,17},{17... | collective-permute-start | bytes 786440 | tf_op jit(solution)/shard_map/while/body/eval_jaxpr/ppermute | solution.py:12
  575.8 10.2 %collective-permute-start = (f32[128,512]{1,0:T(8,128)S(1)}, f32[128,512]{1,0:T(8,128)S(1)}, u32[]{:S(2)}, u32[]{:S(2)}) collective-permute-start(f32[128,512]{1,0:T(8,128)S(1)} %slice.40), channel_id=1, source_target_pairs={{16,0},{32,16},{48,32},{64,48},{80,64},{96,80},{112,96},{17,1},{33... | collective-permute-start | bytes 786440 | tf_op jit(solution)/shard_map/while/body/eval_jaxpr/ppermute | solution.py:12
  587.0 22.6 %collective-permute-start.1 = (f32[128,512]{1,0:T(8,128)S(1)}, f32[128,512]{1,0:T(8,128)S(1)}, u32[]{:S(2)}, u32[]{:S(2)}) collective-permute-start(f32[128,512]{1,0:T(8,128)S(1)} %get-tuple-element.288), channel_id=1, source_target_pairs={{0,16},{16,32},{32,48},{48,64},{64,80},{80,96},{96,112},{1,17},{17... | collective-permute-start | bytes 786440 | tf_op jit(solution)/shard_map/while/body/eval_jaxpr/ppermute | solution.py:12
  611.2 8.3 %collective-permute-start = (f32[128,512]{1,0:T(8,128)S(1)}, f32[128,512]{1,0:T(8,128)S(1)}, u32[]{:S(2)}, u32[]{:S(2)}) collective-permute-start(f32[128,512]{1,0:T(8,128)S(1)} %slice.40), channel_id=1, source_target_pairs={{16,0},{32,16},{48,32},{64,48},{80,64},{96,80},{112,96},{17,1},{33... | collective-permute-start | bytes 786440 | tf_op jit(solution)/shard_map/while/body/eval_jaxpr/ppermute | solution.py:12
  633.9 10.4 %collective-permute-start.1 = (f32[128,512]{1,0:T(8,128)S(1)}, f32[128,512]{1,0:T(8,128)S(1)}, u32[]{:S(2)}, u32[]{:S(2)}) collective-permute-start(f32[128,512]{1,0:T(8,128)S(1)} %get-tuple-element.288), channel_id=1, source_target_pairs={{0,16},{16,32},{32,48},{48,64},{64,80},{80,96},{96,112},{1,17},{17... | collective-permute-start | bytes 786440 | tf_op jit(solution)/shard_map/while/body/eval_jaxpr/ppermute | solution.py:12
  646.1 8.4 %collective-permute-start = (f32[128,512]{1,0:T(8,128)S(1)}, f32[128,512]{1,0:T(8,128)S(1)}, u32[]{:S(2)}, u32[]{:S(2)}) collective-permute-start(f32[128,512]{1,0:T(8,128)S(1)} %slice.40), channel_id=1, source_target_pairs={{16,0},{32,16},{48,32},{64,48},{80,64},{96,80},{112,96},{17,1},{33... | collective-permute-start | bytes 786440 | tf_op jit(solution)/shard_map/while/body/eval_jaxpr/ppermute | solution.py:12
  655.5 22.1 %collective-permute-start.1 = (f32[128,512]{1,0:T(8,128)S(1)}, f32[128,512]{1,0:T(8,128)S(1)}, u32[]{:S(2)}, u32[]{:S(2)}) collective-permute-start(f32[128,512]{1,0:T(8,128)S(1)} %get-tuple-element.288), channel_id=1, source_target_pairs={{0,16},{16,32},{32,48},{48,64},{64,80},{80,96},{96,112},{1,17},{17... | collective-permute-start | bytes 786440 | tf_op jit(solution)/shard_map/while/body/eval_jaxpr/ppermute | solution.py:12
  679.3 8.7 %collective-permute-start = (f32[128,512]{1,0:T(8,128)S(1)}, f32[128,512]{1,0:T(8,128)S(1)}, u32[]{:S(2)}, u32[]{:S(2)}) collective-permute-start(f32[128,512]{1,0:T(8,128)S(1)} %slice.40), channel_id=1, source_target_pairs={{16,0},{32,16},{48,32},{64,48},{80,64},{96,80},{112,96},{17,1},{33... | collective-permute-start | bytes 786440 | tf_op jit(solution)/shard_map/while/body/eval_jaxpr/ppermute | solution.py:12
  702.4 8.3 %collective-permute-start.1 = (f32[128,512]{1,0:T(8,128)S(1)}, f32[128,512]{1,0:T(8,128)S(1)}, u32[]{:S(2)}, u32[]{:S(2)}) collective-permute-start(f32[128,512]{1,0:T(8,128)S(1)} %get-tuple-element.288), channel_id=1, source_target_pairs={{0,16},{16,32},{32,48},{48,64},{64,80},{80,96},{96,112},{1,17},{17... | collective-permute-start | bytes 786440 | tf_op jit(solution)/shard_map/while/body/eval_jaxpr/ppermute | solution.py:12
Sparse Core Ops, SparseCore 0:
  11.4 66.0 all-gather.1
where the time goes:
time: 721 us; the launch traced here: 718 us
  waiting for transfers between devices  375 us (52%)
  starting transfers between devices  154 us (21%)
  matrix products  68.5 us (10%)
  local copies, waits for them, and re-layouts  64.8 us (9%)
  blocking collectives  23.7 us (3%)
  other arithmetic  16.9 us (2%)
  between operations  13.6 us (2%)
    ppermute x36, waiting for transfers between devices, shifted(): return lax.ppermute(block, axis, route)  333 us
    ppermute x36, starting transfers between devices, shifted(): return lax.ppermute(block, axis, route)  154 us
    all_gather x1, waiting for transfers between devices, per_device(): lax.all_gather(mirror_entries, 'col', axis=2, tiled=True)  42 us
    dot_general x6, matrix products, apply_block(): lax.dot_general(mirror_directions, mixed_terms, (((0,), (0,)), ((), ())),...  29.9 us
    all_gather x1, blocking collectives, per_device(): lax.all_gather(tau_coefficients, 'col', axis=2, tiled=True)  23.7 us
    dot_general x6, matrix products, apply_block(): jnp.dot(mirror_directions, window, precision=PRECISE, preferred_element_t...  23.3 us
    slice x18, local copies, waits for them, and re-layouts, advance(): below_rows = shifted(current[:width_rows], 'row', -1)  17.4 us
    cond x6, local copies, waits for them, and re-layouts  15.8 us
  transfers between devices with their start and end apart: 37, of which 37 were waited for; matrix products, arithmetic and copies ran while one was open for 0% of the time, Pallas kernels for 0%

commit v1 on v0

--- a/solution.py
+++ b/solution.py
@@ -56,7 +56,9 @@
 
 def per_device(eigen_basis_rows, mirror_entries, tau_coefficients, mirror_tallies):
     gathered, scale_all = (
-        lax.all_gather(mirror_entries, "col", axis=2, tiled=True),
+        jnp.concatenate(
+            lax.all_to_all(jnp.stack([mirror_entries] * lax.axis_size("col")), "col", 0, 0), axis=2
+        ),
         lax.all_gather(tau_coefficients, "col", axis=2, tiled=True),
     )
     householders = gathered[:, 0]

time: 721 us -> 760 us (1.054)
  blocking collectives: 23.7 us -> 107 us
  waiting for transfers between devices: 375 us -> 332 us
  between operations: 13.6 us -> 0.2 us
  starting transfers between devices: 154 us -> 162 us
    all_gather x1, blocking collectives: 23.7 us -> 107 us  [per_device(): lax.all_gather(tau_coefficients, 'col', axis=2, tiled=True)]
    all_gather x1 -> x0, waiting for transfers between devices: 42 us -> none  [per_device(): lax.all_gather(mirror_entries, 'col', axis=2, tiled=True)]
  transfers between devices with their start and end apart: 37 -> 37, of which waited for: 37 -> 36; matrix products, arithmetic and copies ran while one was open for 0% -> 0% of each run, Pallas kernels for 0% -> 0%
where the time goes in v1:
time: 760 us; the launch traced here: 757 us
  waiting for transfers between devices  332 us (44%)
  starting transfers between devices  162 us (21%)
  blocking collectives  107 us (14%)
  matrix products  68.5 us (9%)
  local copies, waits for them, and re-layouts  68.1 us (9%)
  other arithmetic  16.9 us (2%)
    ppermute x36, waiting for transfers between devices, shifted(): return lax.ppermute(block, axis, route)  332 us
    ppermute x36, starting transfers between devices, shifted(): return lax.ppermute(block, axis, route)  155 us
    all_gather x1, blocking collectives, per_device(): lax.all_gather(tau_coefficients, 'col', axis=2, tiled=True)  107 us
    dot_general x6, matrix products, apply_block(): lax.dot_general(mirror_directions, mixed_terms, (((0,), (0,)), ((), ())),...  29.9 us
    dot_general x6, matrix products, apply_block(): jnp.dot(mirror_directions, window, precision=PRECISE, preferred_element_t...  23.3 us
    slice x18, local copies, waits for them, and re-layouts, advance(): below_rows = shifted(current[:width_rows], 'row', -1)  17.4 us
    cond x6, local copies, waits for them, and re-layouts  15.8 us
  transfers between devices with their start and end apart: 37, of which 36 were waited for; matrix products, arithmetic and copies ran while one was open for 0% of the time, Pallas kernels for 0%

profile of v1, /device:TPU:98, one launch (start us, length us, event | category | flops | bytes accessed | tf_op | source)
XLA Modules:
  0.0 756.9 jit_solution(1854662041044715096)
XLA Ops:
  0.0 4.7 copy.30
  7.9 6.3 all-to-all-start
  14.4 107.5 %all_gather.3 = f32[6,1,128]{0,1,2:T(1,128)S(1)} all-gather(f32[6,1,8]{0,1,2:T(1,128)S(1)} %copy.11), channel_id=1, replica_groups=mesh['row'=8,'col'=16] {'col'}, dimensions={2}, use_global_device_ids=true | all-gather | bytes 3264 | tf_op jit(solution)/shard_map/all_gather | solution.py:62
  125.8 6.6 fusion.13
  138.9 617.9 %while.16 = (s32[]{:T(128)}, f32[2048,512]{1,0:T(8,128)}, s32[]{:T(128)}, f32[6,128,2176]{2,1,0:T(8,128)}, f32[6,128,128]{2,1,0:T(8,128)S(1)}, /*index=5*/s32[]{...) while((s32[]{:T(128)}, f32[2048,512]{1,0:T(8,128)}, s32[]{:T(128)}, ...), condition=%wide.region_3.4_spmd, body=%wide.region_0.3_spmd.sunk | while | flops 3524395008 | bytes 38470408 | solution.py:111
  139.9 8.8 %collective-permute-start = (f32[128,512]{1,0:T(8,128)S(1)}, f32[128,512]{1,0:T(8,128)S(1)}, u32[]{:S(2)}, u32[]{:S(2)}) collective-permute-start(f32[128,512]{1,0:T(8,128)S(1)} %slice.40), channel_id=1, source_target_pairs={{16,0},{32,16},{48,32},{64,48},{80,64},{96,80},{112,96},{17,1},{33... | collective-permute-start | bytes 786440 | tf_op jit(solution)/shard_map/while/body/eval_jaxpr/ppermute | solution.py:12
  148.8 6.0 collective-permute-done
  157.1 9.0 %collective-permute-done.1 = f32[128,512]{1,0:T(8,128)S(1)} collective-permute-done((f32[128,512]{1,0:T(8,128)S(1)}, f32[128,512]{1,0:T(8,128)S(1)}, u32[]{:S(2)}, u32[]{:S(2)}) %collective-permute-start.1) | collective-permute-done | bytes 262176 | tf_op jit(solution)/shard_map/while/body/eval_jaxpr/ppermute | solution.py:12
  167.9 4.6 collective-permute-start
  172.5 4.3 collective-permute-done
  179.1 7.4 collective-permute-done.1
  188.2 4.8 collective-permute-start
  199.2 7.4 collective-permute-done.1
  208.3 4.8 collective-permute-start
  219.4 11.7 %collective-permute-done.1 = f32[128,512]{1,0:T(8,128)S(1)} collective-permute-done((f32[128,512]{1,0:T(8,128)S(1)}, f32[128,512]{1,0:T(8,128)S(1)}, u32[]{:S(2)}, u32[]{:S(2)}) %collective-permute-start.1) | collective-permute-done | bytes 262176 | tf_op jit(solution)/shard_map/while/body/eval_jaxpr/ppermute | solution.py:12
  232.8 18.7 %collective-permute-start = (f32[128,512]{1,0:T(8,128)S(1)}, f32[128,512]{1,0:T(8,128)S(1)}, u32[]{:S(2)}, u32[]{:S(2)}) collective-permute-start(f32[128,512]{1,0:T(8,128)S(1)} %slice.40), channel_id=1, source_target_pairs={{16,0},{32,16},{48,32},{64,48},{80,64},{96,80},{112,96},{17,1},{33... | collective-permute-start | bytes 786440 | tf_op jit(solution)/shard_map/while/body/eval_jaxpr/ppermute | solution.py:12
  251.6 3.8 collective-permute-done
  257.7 22.9 %collective-permute-done.1 = f32[128,512]{1,0:T(8,128)S(1)} collective-permute-done((f32[128,512]{1,0:T(8,128)S(1)}, f32[128,512]{1,0:T(8,128)S(1)}, u32[]{:S(2)}, u32[]{:S(2)}) %collective-permute-start.1) | collective-permute-done | bytes 262176 | tf_op jit(solution)/shard_map/while/body/eval_jaxpr/ppermute | solution.py:12
  282.3 19.2 %collective-permute-start = (f32[128,512]{1,0:T(8,128)S(1)}, f32[128,512]{1,0:T(8,128)S(1)}, u32[]{:S(2)}, u32[]{:S(2)}) collective-permute-start(f32[128,512]{1,0:T(8,128)S(1)} %slice.40), channel_id=1, source_target_pairs={{16,0},{32,16},{48,32},{64,48},{80,64},{96,80},{112,96},{17,1},{33... | collective-permute-start | bytes 786440 | tf_op jit(solution)/shard_map/while/body/eval_jaxpr/ppermute | solution.py:12
  307.7 22.4 %collective-permute-done.1 = f32[128,512]{1,0:T(8,128)S(1)} collective-permute-done((f32[128,512]{1,0:T(8,128)S(1)}, f32[128,512]{1,0:T(8,128)S(1)}, u32[]{:S(2)}, u32[]{:S(2)}) %collective-permute-start.1) | collective-permute-done | bytes 262176 | tf_op jit(solution)/shard_map/while/body/eval_jaxpr/ppermute | solution.py:12
  331.8 18.7 %collective-permute-start = (f32[128,512]{1,0:T(8,128)S(1)}, f32[128,512]{1,0:T(8,128)S(1)}, u32[]{:S(2)}, u32[]{:S(2)}) collective-permute-start(f32[128,512]{1,0:T(8,128)S(1)} %slice.40), channel_id=1, source_target_pairs={{16,0},{32,16},{48,32},{64,48},{80,64},{96,80},{112,96},{17,1},{33... | collective-permute-start | bytes 786440 | tf_op jit(solution)/shard_map/while/body/eval_jaxpr/ppermute | solution.py:12
  356.7 20.8 %collective-permute-done.1 = f32[128,512]{1,0:T(8,128)S(1)} collective-permute-done((f32[128,512]{1,0:T(8,128)S(1)}, f32[128,512]{1,0:T(8,128)S(1)}, u32[]{:S(2)}, u32[]{:S(2)}) %collective-permute-start.1) | collective-permute-done | bytes 262176 | tf_op jit(solution)/shard_map/while/body/eval_jaxpr/ppermute | solution.py:12
  379.2 4.8 collective-permute-start
  387.9 14.4 %conditional.2 = (f32[2048,512]{1,0:T(8,128)}, f32[128,512]{1,0:T(8,128)S(1)}, f32[128,512]{1,0:T(8,128)S(1)}) conditional(s32[]{:T(128)} %convert_element_type.41, (f32[2048,512]{1,0:T(8,128)}, f32[128,512]{1,0:T(8,128)S(1)}) %tuple.59, (f32[2048,512]{1,0:T(8,128)}, f32[128,512]{1,0:T(8,128)S(1)}, s32[]{:T(128)}, f32[6,128,2176]{2,1,0:T(8,128)}, ...), branch_computations={%region_1.1_spmd, %region_2.2_spmd} | conditional | flops 3524329472 | bytes 35061820 | solution.py:104
  390.6 3.9 fusion.1
  394.8 5.0 convolution_subtract_fusion
  403.7 6.9 collective-permute-done.1
  412.3 4.8 collective-permute-start
  423.2 23.0 %collective-permute-done.1 = f32[128,512]{1,0:T(8,128)S(1)} collective-permute-done((f32[128,512]{1,0:T(8,128)S(1)}, f32[128,512]{1,0:T(8,128)S(1)}, u32[]{:S(2)}, u32[]{:S(2)}) %collective-permute-start.1) | collective-permute-done | bytes 262176 | tf_op jit(solution)/shard_map/while/body/eval_jaxpr/ppermute | solution.py:12
  448.0 4.8 collective-permute-start
  456.7 14.4 %conditional.2 = (f32[2048,512]{1,0:T(8,128)}, f32[128,512]{1,0:T(8,128)S(1)}, f32[128,512]{1,0:T(8,128)S(1)}) conditional(s32[]{:T(128)} %convert_element_type.41, (f32[2048,512]{1,0:T(8,128)}, f32[128,512]{1,0:T(8,128)S(1)}) %tuple.59, (f32[2048,512]{1,0:T(8,128)}, f32[128,512]{1,0:T(8,128)S(1)}, s32[]{:T(128)}, f32[6,128,2176]{2,1,0:T(8,128)}, ...), branch_computations={%region_1.1_spmd, %region_2.2_spmd} | conditional | flops 3524329472 | bytes 35061820 | solution.py:104
  459.3 3.9 fusion.1
  463.6 5.0 convolution_subtract_fusion
  472.4 6.9 collective-permute-done.1
  490.6 20.8 %collective-permute-done.1 = f32[128,512]{1,0:T(8,128)S(1)} collective-permute-done((f32[128,512]{1,0:T(8,128)S(1)}, f32[128,512]{1,0:T(8,128)S(1)}, u32[]{:S(2)}, u32[]{:S(2)}) %collective-permute-start.1) | collective-permute-done | bytes 262176 | tf_op jit(solution)/shard_map/while/body/eval_jaxpr/ppermute | solution.py:12
  513.1 4.8 collective-permute-start
  521.8 14.4 %conditional.2 = (f32[2048,512]{1,0:T(8,128)}, f32[128,512]{1,0:T(8,128)S(1)}, f32[128,512]{1,0:T(8,128)S(1)}) conditional(s32[]{:T(128)} %convert_element_type.41, (f32[2048,512]{1,0:T(8,128)}, f32[128,512]{1,0:T(8,128)S(1)}) %tuple.59, (f32[2048,512]{1,0:T(8,128)}, f32[128,512]{1,0:T(8,128)S(1)}, s32[]{:T(128)}, f32[6,128,2176]{2,1,0:T(8,128)}, ...), branch_computations={%region_1.1_spmd, %region_2.2_spmd} | conditional | flops 3524329472 | bytes 35061820 | solution.py:104
  524.5 3.9 fusion.1
  528.7 5.0 convolution_subtract_fusion
  537.5 6.9 collective-permute-done.1
  546.2 5.5 collective-permute-start
  557.9 20.8 %collective-permute-done.1 = f32[128,512]{1,0:T(8,128)S(1)} collective-permute-done((f32[128,512]{1,0:T(8,128)S(1)}, f32[128,512]{1,0:T(8,128)S(1)}, u32[]{:S(2)}, u32[]{:S(2)}) %collective-permute-start.1) | collective-permute-done | bytes 262176 | tf_op jit(solution)/shard_map/while/body/eval_jaxpr/ppermute | solution.py:12
  580.4 4.8 collective-permute-start
  585.3 4.1 collective-permute-done
  589.4 14.4 %conditional.2 = (f32[2048,512]{1,0:T(8,128)}, f32[128,512]{1,0:T(8,128)S(1)}, f32[128,512]{1,0:T(8,128)S(1)}) conditional(s32[]{:T(128)} %convert_element_type.41, (f32[2048,512]{1,0:T(8,128)}, f32[128,512]{1,0:T(8,128)S(1)}) %tuple.59, (f32[2048,512]{1,0:T(8,128)}, f32[128,512]{1,0:T(8,128)S(1)}, s32[]{:T(128)}, f32[6,128,2176]{2,1,0:T(8,128)}, ...), branch_computations={%region_1.1_spmd, %region_2.2_spmd} | conditional | flops 3524329472 | bytes 35061820 | solution.py:104
  592.1 3.9 fusion.1
  596.4 5.0 convolution_subtract_fusion
  605.2 7.6 collective-permute-done.1
  618.3 5.2 collective-permute-done
  625.8 23.8 %collective-permute-done.1 = f32[128,512]{1,0:T(8,128)S(1)} collective-permute-done((f32[128,512]{1,0:T(8,128)S(1)}, f32[128,512]{1,0:T(8,128)S(1)}, u32[]{:S(2)}, u32[]{:S(2)}) %collective-permute-start.1) | collective-permute-done | bytes 262176 | tf_op jit(solution)/shard_map/while/body/eval_jaxpr/ppermute | solution.py:12
  651.2 6.6 collective-permute-start
  657.9 5.7 collective-permute-done
  663.6 14.4 %conditional.2 = (f32[2048,512]{1,0:T(8,128)}, f32[128,512]{1,0:T(8,128)S(1)}, f32[128,512]{1,0:T(8,128)S(1)}) conditional(s32[]{:T(128)} %convert_element_type.41, (f32[2048,512]{1,0:T(8,128)}, f32[128,512]{1,0:T(8,128)S(1)}) %tuple.59, (f32[2048,512]{1,0:T(8,128)}, f32[128,512]{1,0:T(8,128)S(1)}, s32[]{:T(128)}, f32[6,128,2176]{2,1,0:T(8,128)}, ...), branch_computations={%region_1.1_spmd, %region_2.2_spmd} | conditional | flops 3524329472 | bytes 35061820 | solution.py:104
  666.3 3.9 fusion.1
  670.5 5.0 convolution_subtract_fusion
  679.3 8.7 %collective-permute-done.1 = f32[128,512]{1,0:T(8,128)S(1)} collective-permute-done((f32[128,512]{1,0:T(8,128)S(1)}, f32[128,512]{1,0:T(8,128)S(1)}, u32[]{:S(2)}, u32[]{:S(2)}) %collective-permute-start.1) | collective-permute-done | bytes 262176 | tf_op jit(solution)/shard_map/while/body/eval_jaxpr/ppermute | solution.py:12
  689.7 4.6 collective-permute-start
  694.3 5.6 collective-permute-done
  702.3 21.3 %collective-permute-done.1 = f32[128,512]{1,0:T(8,128)S(1)} collective-permute-done((f32[128,512]{1,0:T(8,128)S(1)}, f32[128,512]{1,0:T(8,128)S(1)}, u32[]{:S(2)}, u32[]{:S(2)}) %collective-permute-start.1) | collective-permute-done | bytes 262176 | tf_op jit(solution)/shard_map/while/body/eval_jaxpr/ppermute | solution.py:12
  725.3 4.4 collective-permute-start
  733.5 14.4 %conditional.2 = (f32[2048,512]{1,0:T(8,128)}, f32[128,512]{1,0:T(8,128)S(1)}, f32[128,512]{1,0:T(8,128)S(1)}) conditional(s32[]{:T(128)} %convert_element_type.41, (f32[2048,512]{1,0:T(8,128)}, f32[128,512]{1,0:T(8,128)S(1)}) %tuple.59, (f32[2048,512]{1,0:T(8,128)}, f32[128,512]{1,0:T(8,128)S(1)}, s32[]{:T(128)}, f32[6,128,2176]{2,1,0:T(8,128)}, ...), branch_computations={%region_1.1_spmd, %region_2.2_spmd} | conditional | flops 3524329472 | bytes 35061820 | solution.py:104
  736.1 3.9 fusion.1
  740.4 5.0 convolution_subtract_fusion
  749.2 6.9 collective-permute-done.1
  (154 shorter events, 173.0 us)
Async XLA Ops:
  0.0 4.7 copy-start.1
  7.9 6.3 copy-start.2
  7.9 6.4 copy-start.3
  7.9 114.3 %all-to-all-start = ((f32[16,6,1,8,2176]{4,3,1,2,0:T(8,128)}), f32[16,6,1,8,2176]{4,3,1,2,0:T(8,128)}, u32[]{:S(2)}, u32[]{:S(2)}) async-start(f32[16,6,1,8,2176]{4,3,1,2,0:T(8,128)} %stack.2), calls=%async_computation | async-start | bytes 13369344 | tf_op jit(solution)/shard_map/all_to_all | solution.py:60
  125.7 6.6 copy-start
  139.9 14.9 %collective-permute-start = (f32[128,512]{1,0:T(8,128)S(1)}, f32[128,512]{1,0:T(8,128)S(1)}, u32[]{:S(2)}, u32[]{:S(2)}) collective-permute-start(f32[128,512]{1,0:T(8,128)S(1)} %slice.40), channel_id=1, source_target_pairs={{16,0},{32,16},{48,32},{64,48},{80,64},{96,80},{112,96},{17,1},{33... | collective-permute-start | bytes 786440 | tf_op jit(solution)/shard_map/while/body/eval_jaxpr/ppermute | solution.py:12
  155.8 10.4 %collective-permute-start.1 = (f32[128,512]{1,0:T(8,128)S(1)}, f32[128,512]{1,0:T(8,128)S(1)}, u32[]{:S(2)}, u32[]{:S(2)}) collective-permute-start(f32[128,512]{1,0:T(8,128)S(1)} %get-tuple-element.288), channel_id=1, source_target_pairs={{0,16},{16,32},{32,48},{48,64},{64,80},{80,96},{96,112},{1,17},{17... | collective-permute-start | bytes 786440 | tf_op jit(solution)/shard_map/while/body/eval_jaxpr/ppermute | solution.py:12
  167.9 8.9 %collective-permute-start = (f32[128,512]{1,0:T(8,128)S(1)}, f32[128,512]{1,0:T(8,128)S(1)}, u32[]{:S(2)}, u32[]{:S(2)}) collective-permute-start(f32[128,512]{1,0:T(8,128)S(1)} %slice.40), channel_id=1, source_target_pairs={{16,0},{32,16},{48,32},{64,48},{80,64},{96,80},{112,96},{17,1},{33... | collective-permute-start | bytes 786440 | tf_op jit(solution)/shard_map/while/body/eval_jaxpr/ppermute | solution.py:12
  177.8 8.7 %collective-permute-start.1 = (f32[128,512]{1,0:T(8,128)S(1)}, f32[128,512]{1,0:T(8,128)S(1)}, u32[]{:S(2)}, u32[]{:S(2)}) collective-permute-start(f32[128,512]{1,0:T(8,128)S(1)} %get-tuple-element.288), channel_id=1, source_target_pairs={{0,16},{16,32},{32,48},{48,64},{64,80},{80,96},{96,112},{1,17},{17... | collective-permute-start | bytes 786440 | tf_op jit(solution)/shard_map/while/body/eval_jaxpr/ppermute | solution.py:12
  188.2 8.7 %collective-permute-start = (f32[128,512]{1,0:T(8,128)S(1)}, f32[128,512]{1,0:T(8,128)S(1)}, u32[]{:S(2)}, u32[]{:S(2)}) collective-permute-start(f32[128,512]{1,0:T(8,128)S(1)} %slice.40), channel_id=1, source_target_pairs={{16,0},{32,16},{48,32},{64,48},{80,64},{96,80},{112,96},{17,1},{33... | collective-permute-start | bytes 786440 | tf_op jit(solution)/shard_map/while/body/eval_jaxpr/ppermute | solution.py:12
  197.9 8.7 %collective-permute-start.1 = (f32[128,512]{1,0:T(8,128)S(1)}, f32[128,512]{1,0:T(8,128)S(1)}, u32[]{:S(2)}, u32[]{:S(2)}) collective-permute-start(f32[128,512]{1,0:T(8,128)S(1)} %get-tuple-element.288), channel_id=1, source_target_pairs={{0,16},{16,32},{32,48},{48,64},{64,80},{80,96},{96,112},{1,17},{17... | collective-permute-start | bytes 786440 | tf_op jit(solution)/shard_map/while/body/eval_jaxpr/ppermute | solution.py:12
  208.3 8.7 %collective-permute-start = (f32[128,512]{1,0:T(8,128)S(1)}, f32[128,512]{1,0:T(8,128)S(1)}, u32[]{:S(2)}, u32[]{:S(2)}) collective-permute-start(f32[128,512]{1,0:T(8,128)S(1)} %slice.40), channel_id=1, source_target_pairs={{16,0},{32,16},{48,32},{64,48},{80,64},{96,80},{112,96},{17,1},{33... | collective-permute-start | bytes 786440 | tf_op jit(solution)/shard_map/while/body/eval_jaxpr/ppermute | solution.py:12
  218.0 13.1 %collective-permute-start.1 = (f32[128,512]{1,0:T(8,128)S(1)}, f32[128,512]{1,0:T(8,128)S(1)}, u32[]{:S(2)}, u32[]{:S(2)}) collective-permute-start(f32[128,512]{1,0:T(8,128)S(1)} %get-tuple-element.288), channel_id=1, source_target_pairs={{0,16},{16,32},{32,48},{48,64},{64,80},{80,96},{96,112},{1,17},{17... | collective-permute-start | bytes 786440 | tf_op jit(solution)/shard_map/while/body/eval_jaxpr/ppermute | solution.py:12
  232.8 22.6 %collective-permute-start = (f32[128,512]{1,0:T(8,128)S(1)}, f32[128,512]{1,0:T(8,128)S(1)}, u32[]{:S(2)}, u32[]{:S(2)}) collective-permute-start(f32[128,512]{1,0:T(8,128)S(1)} %slice.40), channel_id=1, source_target_pairs={{16,0},{32,16},{48,32},{64,48},{80,64},{96,80},{112,96},{17,1},{33... | collective-permute-start | bytes 786440 | tf_op jit(solution)/shard_map/while/body/eval_jaxpr/ppermute | solution.py:12
  256.4 24.2 %collective-permute-start.1 = (f32[128,512]{1,0:T(8,128)S(1)}, f32[128,512]{1,0:T(8,128)S(1)}, u32[]{:S(2)}, u32[]{:S(2)}) collective-permute-start(f32[128,512]{1,0:T(8,128)S(1)} %get-tuple-element.288), channel_id=1, source_target_pairs={{0,16},{16,32},{32,48},{48,64},{64,80},{80,96},{96,112},{1,17},{17... | collective-permute-start | bytes 786440 | tf_op jit(solution)/shard_map/while/body/eval_jaxpr/ppermute | solution.py:12
  282.3 23.1 %collective-permute-start = (f32[128,512]{1,0:T(8,128)S(1)}, f32[128,512]{1,0:T(8,128)S(1)}, u32[]{:S(2)}, u32[]{:S(2)}) collective-permute-start(f32[128,512]{1,0:T(8,128)S(1)} %slice.40), channel_id=1, source_target_pairs={{16,0},{32,16},{48,32},{64,48},{80,64},{96,80},{112,96},{17,1},{33... | collective-permute-start | bytes 786440 | tf_op jit(solution)/shard_map/while/body/eval_jaxpr/ppermute | solution.py:12
  306.4 23.7 %collective-permute-start.1 = (f32[128,512]{1,0:T(8,128)S(1)}, f32[128,512]{1,0:T(8,128)S(1)}, u32[]{:S(2)}, u32[]{:S(2)}) collective-permute-start(f32[128,512]{1,0:T(8,128)S(1)} %get-tuple-element.288), channel_id=1, source_target_pairs={{0,16},{16,32},{32,48},{48,64},{64,80},{80,96},{96,112},{1,17},{17... | collective-permute-start | bytes 786440 | tf_op jit(solution)/shard_map/while/body/eval_jaxpr/ppermute | solution.py:12
  331.8 22.6 %collective-permute-start = (f32[128,512]{1,0:T(8,128)S(1)}, f32[128,512]{1,0:T(8,128)S(1)}, u32[]{:S(2)}, u32[]{:S(2)}) collective-permute-start(f32[128,512]{1,0:T(8,128)S(1)} %slice.40), channel_id=1, source_target_pairs={{16,0},{32,16},{48,32},{64,48},{80,64},{96,80},{112,96},{17,1},{33... | collective-permute-start | bytes 786440 | tf_op jit(solution)/shard_map/while/body/eval_jaxpr/ppermute | solution.py:12
  355.4 22.2 %collective-permute-start.1 = (f32[128,512]{1,0:T(8,128)S(1)}, f32[128,512]{1,0:T(8,128)S(1)}, u32[]{:S(2)}, u32[]{:S(2)}) collective-permute-start(f32[128,512]{1,0:T(8,128)S(1)} %get-tuple-element.288), channel_id=1, source_target_pairs={{0,16},{16,32},{32,48},{48,64},{64,80},{80,96},{96,112},{1,17},{17... | collective-permute-start | bytes 786440 | tf_op jit(solution)/shard_map/while/body/eval_jaxpr/ppermute | solution.py:12
  379.2 8.7 %collective-permute-start = (f32[128,512]{1,0:T(8,128)S(1)}, f32[128,512]{1,0:T(8,128)S(1)}, u32[]{:S(2)}, u32[]{:S(2)}) collective-permute-start(f32[128,512]{1,0:T(8,128)S(1)} %slice.40), channel_id=1, source_target_pairs={{16,0},{32,16},{48,32},{64,48},{80,64},{96,80},{112,96},{17,1},{33... | collective-permute-start | bytes 786440 | tf_op jit(solution)/shard_map/while/body/eval_jaxpr/ppermute | solution.py:12
  402.3 8.3 %collective-permute-start.1 = (f32[128,512]{1,0:T(8,128)S(1)}, f32[128,512]{1,0:T(8,128)S(1)}, u32[]{:S(2)}, u32[]{:S(2)}) collective-permute-start(f32[128,512]{1,0:T(8,128)S(1)} %get-tuple-element.288), channel_id=1, source_target_pairs={{0,16},{16,32},{32,48},{48,64},{64,80},{80,96},{96,112},{1,17},{17... | collective-permute-start | bytes 786440 | tf_op jit(solution)/shard_map/while/body/eval_jaxpr/ppermute | solution.py:12
  412.3 8.6 %collective-permute-start = (f32[128,512]{1,0:T(8,128)S(1)}, f32[128,512]{1,0:T(8,128)S(1)}, u32[]{:S(2)}, u32[]{:S(2)}) collective-permute-start(f32[128,512]{1,0:T(8,128)S(1)} %slice.40), channel_id=1, source_target_pairs={{16,0},{32,16},{48,32},{64,48},{80,64},{96,80},{112,96},{17,1},{33... | collective-permute-start | bytes 786440 | tf_op jit(solution)/shard_map/while/body/eval_jaxpr/ppermute | solution.py:12
  421.9 24.4 %collective-permute-start.1 = (f32[128,512]{1,0:T(8,128)S(1)}, f32[128,512]{1,0:T(8,128)S(1)}, u32[]{:S(2)}, u32[]{:S(2)}) collective-permute-start(f32[128,512]{1,0:T(8,128)S(1)} %get-tuple-element.288), channel_id=1, source_target_pairs={{0,16},{16,32},{32,48},{48,64},{64,80},{80,96},{96,112},{1,17},{17... | collective-permute-start | bytes 786440 | tf_op jit(solution)/shard_map/while/body/eval_jaxpr/ppermute | solution.py:12
  448.0 8.7 %collective-permute-start = (f32[128,512]{1,0:T(8,128)S(1)}, f32[128,512]{1,0:T(8,128)S(1)}, u32[]{:S(2)}, u32[]{:S(2)}) collective-permute-start(f32[128,512]{1,0:T(8,128)S(1)} %slice.40), channel_id=1, source_target_pairs={{16,0},{32,16},{48,32},{64,48},{80,64},{96,80},{112,96},{17,1},{33... | collective-permute-start | bytes 786440 | tf_op jit(solution)/shard_map/while/body/eval_jaxpr/ppermute | solution.py:12
  471.1 8.3 %collective-permute-start.1 = (f32[128,512]{1,0:T(8,128)S(1)}, f32[128,512]{1,0:T(8,128)S(1)}, u32[]{:S(2)}, u32[]{:S(2)}) collective-permute-start(f32[128,512]{1,0:T(8,128)S(1)} %get-tuple-element.288), channel_id=1, source_target_pairs={{0,16},{16,32},{32,48},{48,64},{64,80},{80,96},{96,112},{1,17},{17... | collective-permute-start | bytes 786440 | tf_op jit(solution)/shard_map/while/body/eval_jaxpr/ppermute | solution.py:12
  481.0 7.2 collective-permute-start
  489.2 22.2 %collective-permute-start.1 = (f32[128,512]{1,0:T(8,128)S(1)}, f32[128,512]{1,0:T(8,128)S(1)}, u32[]{:S(2)}, u32[]{:S(2)}) collective-permute-start(f32[128,512]{1,0:T(8,128)S(1)} %get-tuple-element.288), channel_id=1, source_target_pairs={{0,16},{16,32},{32,48},{48,64},{64,80},{80,96},{96,112},{1,17},{17... | collective-permute-start | bytes 786440 | tf_op jit(solution)/shard_map/while/body/eval_jaxpr/ppermute | solution.py:12
  513.1 8.7 %collective-permute-start = (f32[128,512]{1,0:T(8,128)S(1)}, f32[128,512]{1,0:T(8,128)S(1)}, u32[]{:S(2)}, u32[]{:S(2)}) collective-permute-start(f32[128,512]{1,0:T(8,128)S(1)} %slice.40), channel_id=1, source_target_pairs={{16,0},{32,16},{48,32},{64,48},{80,64},{96,80},{112,96},{17,1},{33... | collective-permute-start | bytes 786440 | tf_op jit(solution)/shard_map/while/body/eval_jaxpr/ppermute | solution.py:12
  536.2 8.3 %collective-permute-start.1 = (f32[128,512]{1,0:T(8,128)S(1)}, f32[128,512]{1,0:T(8,128)S(1)}, u32[]{:S(2)}, u32[]{:S(2)}) collective-permute-start(f32[128,512]{1,0:T(8,128)S(1)} %get-tuple-element.288), channel_id=1, source_target_pairs={{0,16},{16,32},{32,48},{48,64},{64,80},{80,96},{96,112},{1,17},{17... | collective-permute-start | bytes 786440 | tf_op jit(solution)/shard_map/while/body/eval_jaxpr/ppermute | solution.py:12
  546.2 9.4 %collective-permute-start = (f32[128,512]{1,0:T(8,128)S(1)}, f32[128,512]{1,0:T(8,128)S(1)}, u32[]{:S(2)}, u32[]{:S(2)}) collective-permute-start(f32[128,512]{1,0:T(8,128)S(1)} %slice.40), channel_id=1, source_target_pairs={{16,0},{32,16},{48,32},{64,48},{80,64},{96,80},{112,96},{17,1},{33... | collective-permute-start | bytes 786440 | tf_op jit(solution)/shard_map/while/body/eval_jaxpr/ppermute | solution.py:12
  556.6 22.2 %collective-permute-start.1 = (f32[128,512]{1,0:T(8,128)S(1)}, f32[128,512]{1,0:T(8,128)S(1)}, u32[]{:S(2)}, u32[]{:S(2)}) collective-permute-start(f32[128,512]{1,0:T(8,128)S(1)} %get-tuple-element.288), channel_id=1, source_target_pairs={{0,16},{16,32},{32,48},{48,64},{64,80},{80,96},{96,112},{1,17},{17... | collective-permute-start | bytes 786440 | tf_op jit(solution)/shard_map/while/body/eval_jaxpr/ppermute | solution.py:12
  580.4 9.0 %collective-permute-start = (f32[128,512]{1,0:T(8,128)S(1)}, f32[128,512]{1,0:T(8,128)S(1)}, u32[]{:S(2)}, u32[]{:S(2)}) collective-permute-start(f32[128,512]{1,0:T(8,128)S(1)} %slice.40), channel_id=1, source_target_pairs={{16,0},{32,16},{48,32},{64,48},{80,64},{96,80},{112,96},{17,1},{33... | collective-permute-start | bytes 786440 | tf_op jit(solution)/shard_map/while/body/eval_jaxpr/ppermute | solution.py:12
  603.8 8.9 %collective-permute-start.1 = (f32[128,512]{1,0:T(8,128)S(1)}, f32[128,512]{1,0:T(8,128)S(1)}, u32[]{:S(2)}, u32[]{:S(2)}) collective-permute-start(f32[128,512]{1,0:T(8,128)S(1)} %get-tuple-element.288), channel_id=1, source_target_pairs={{0,16},{16,32},{32,48},{48,64},{64,80},{80,96},{96,112},{1,17},{17... | collective-permute-start | bytes 786440 | tf_op jit(solution)/shard_map/while/body/eval_jaxpr/ppermute | solution.py:12
  614.4 9.0 %collective-permute-start = (f32[128,512]{1,0:T(8,128)S(1)}, f32[128,512]{1,0:T(8,128)S(1)}, u32[]{:S(2)}, u32[]{:S(2)}) collective-permute-start(f32[128,512]{1,0:T(8,128)S(1)} %slice.40), channel_id=1, source_target_pairs={{16,0},{32,16},{48,32},{64,48},{80,64},{96,80},{112,96},{17,1},{33... | collective-permute-start | bytes 786440 | tf_op jit(solution)/shard_map/while/body/eval_jaxpr/ppermute | solution.py:12
  624.4 25.1 %collective-permute-start.1 = (f32[128,512]{1,0:T(8,128)S(1)}, f32[128,512]{1,0:T(8,128)S(1)}, u32[]{:S(2)}, u32[]{:S(2)}) collective-permute-start(f32[128,512]{1,0:T(8,128)S(1)} %get-tuple-element.288), channel_id=1, source_target_pairs={{0,16},{16,32},{32,48},{48,64},{64,80},{80,96},{96,112},{1,17},{17... | collective-permute-start | bytes 786440 | tf_op jit(solution)/shard_map/while/body/eval_jaxpr/ppermute | solution.py:12
  651.2 12.3 %collective-permute-start = (f32[128,512]{1,0:T(8,128)S(1)}, f32[128,512]{1,0:T(8,128)S(1)}, u32[]{:S(2)}, u32[]{:S(2)}) collective-permute-start(f32[128,512]{1,0:T(8,128)S(1)} %slice.40), channel_id=1, source_target_pairs={{16,0},{32,16},{48,32},{64,48},{80,64},{96,80},{112,96},{17,1},{33... | collective-permute-start | bytes 786440 | tf_op jit(solution)/shard_map/while/body/eval_jaxpr/ppermute | solution.py:12
  678.0 10.0 %collective-permute-start.1 = (f32[128,512]{1,0:T(8,128)S(1)}, f32[128,512]{1,0:T(8,128)S(1)}, u32[]{:S(2)}, u32[]{:S(2)}) collective-permute-start(f32[128,512]{1,0:T(8,128)S(1)} %get-tuple-element.288), channel_id=1, source_target_pairs={{0,16},{16,32},{32,48},{48,64},{64,80},{80,96},{96,112},{1,17},{17... | collective-permute-start | bytes 786440 | tf_op jit(solution)/shard_map/while/body/eval_jaxpr/ppermute | solution.py:12
  689.7 10.2 %collective-permute-start = (f32[128,512]{1,0:T(8,128)S(1)}, f32[128,512]{1,0:T(8,128)S(1)}, u32[]{:S(2)}, u32[]{:S(2)}) collective-permute-start(f32[128,512]{1,0:T(8,128)S(1)} %slice.40), channel_id=1, source_target_pairs={{16,0},{32,16},{48,32},{64,48},{80,64},{96,80},{112,96},{17,1},{33... | collective-permute-start | bytes 786440 | tf_op jit(solution)/shard_map/while/body/eval_jaxpr/ppermute | solution.py:12
  700.9 22.6 %collective-permute-start.1 = (f32[128,512]{1,0:T(8,128)S(1)}, f32[128,512]{1,0:T(8,128)S(1)}, u32[]{:S(2)}, u32[]{:S(2)}) collective-permute-start(f32[128,512]{1,0:T(8,128)S(1)} %get-tuple-element.288), channel_id=1, source_target_pairs={{0,16},{16,32},{32,48},{48,64},{64,80},{80,96},{96,112},{1,17},{17... | collective-permute-start | bytes 786440 | tf_op jit(solution)/shard_map/while/body/eval_jaxpr/ppermute | solution.py:12
  725.3 8.2 %collective-permute-start = (f32[128,512]{1,0:T(8,128)S(1)}, f32[128,512]{1,0:T(8,128)S(1)}, u32[]{:S(2)}, u32[]{:S(2)}) collective-permute-start(f32[128,512]{1,0:T(8,128)S(1)} %slice.40), channel_id=1, source_target_pairs={{16,0},{32,16},{48,32},{64,48},{80,64},{96,80},{112,96},{17,1},{33... | collective-permute-start | bytes 786440 | tf_op jit(solution)/shard_map/while/body/eval_jaxpr/ppermute | solution.py:12
  747.9 8.3 %collective-permute-start.1 = (f32[128,512]{1,0:T(8,128)S(1)}, f32[128,512]{1,0:T(8,128)S(1)}, u32[]{:S(2)}, u32[]{:S(2)}) collective-permute-start(f32[128,512]{1,0:T(8,128)S(1)} %get-tuple-element.288), channel_id=1, source_target_pairs={{0,16},{16,32},{32,48},{48,64},{64,80},{80,96},{96,112},{1,17},{17... | collective-permute-start | bytes 786440 | tf_op jit(solution)/shard_map/while/body/eval_jaxpr/ppermute | solution.py:12
